TPU v7x, 32 devices: a whole 2x2x4 slice. The times are simulated.
32 devices in a mesh: shard: 8 (over y, x, core), replica: 4 (over z).
Axes of the slice: x: 2, y: 2, z: 4, core: 2. Of those that a mesh axis runs over, the one named last changes fastest.
Arguments:
- grads: bfloat16 [4, 32, 256, 256], P('replica', None, 'shard')
- table: int32 [32], replicated, may hold values from 0 to 31, each once
- left_code: bfloat16 [32, 256, 256], P(('shard', 'replica')), may hold values from -7 to 7, as said below
- left_scale: float32 [32, 2, 256], P(('shard', 'replica')), may hold values from 0.2 to 2
- right_code: bfloat16 [32, 256, 256], P(('shard', 'replica')), may hold values from -7 to 7, as said below
- right_scale: float32 [32, 2, 256], P(('shard', 'replica')), may hold values from 0.2 to 2
- left_root_code: bfloat16 [32, 256, 256], P(('shard', 'replica')), may hold values from -7 to 7, as said below
- left_root_scale: float32 [32, 2, 256], P(('shard', 'replica')), may hold values from 0.01 to 0.1
- right_root_code: bfloat16 [32, 256, 256], P(('shard', 'replica')), may hold values from -7 to 7, as said below
- right_root_scale: float32 [32, 2, 256], P(('shard', 'replica')), may hold values from 0.01 to 0.1
Outputs:
- direction: bfloat16 [32, 256, 256], P(None, 'shard')
- new_left: bfloat16 [32, 256, 256], P(('shard', 'replica'))
- new_left_scale: float32 [32, 2, 256], P(('shard', 'replica'))
- new_right: bfloat16 [32, 256, 256], P(('shard', 'replica'))
- new_right_scale: float32 [32, 2, 256], P(('shard', 'replica'))
Inputs may be any that keep to these rules, and one draw needn't show every extreme that they name: `table`: a permutation: every block is held by exactly one slot. `left_code`: whole numbers. `right_code`: whole numbers. `left_root_code`: whole numbers. `right_root_code`: whole numbers.
All inputs are finite; a program needn't handle non-finite values.
Results may differ from a plain program's by a relative error of at most 0.012.
Values may be sent and summed in bfloat16 or wider, within the bound.
A program may use at most 64 MiB of HBM per device.

v0:
```python
import jax
import jax.numpy as jnp
from jax import lax
from jax.sharding import PartitionSpec as P

QG = 128


DECAY = 0.9
EPSILON = 1e-06


def dequantize(code_block, scale_grid):
    count, height, breadth = code_block.shape
    grouped = code_block.astype(jnp.float32).reshape(count, height, breadth // QG, QG)
    return (grouped * jnp.swapaxes(scale_grid, 1, 2)[..., None]).reshape(count, height, breadth)


def requantize(matrix):
    count, height, breadth = matrix.shape
    grouped = matrix.reshape(count, height, breadth // QG, QG)
    largest = jnp.max(jnp.abs(grouped), axis=3)
    step_size = (largest + EPSILON) / 7.0
    values = (grouped / step_size[..., None]).reshape(count, height, breadth).astype(jnp.bfloat16)
    return (values, jnp.swapaxes(step_size, 1, 2))


def precondition(
    summed,
    left_code,
    left_scale,
    right_code,
    right_scale,
    left_root_code,
    left_root_scale,
    right_root_code,
    right_root_scale,
):
    highest = lax.Precision.HIGHEST
    left = dequantize(left_code, left_scale)
    right = dequantize(right_code, right_scale)
    left_root = dequantize(left_root_code, left_root_scale)
    right_root = dequantize(right_root_code, right_root_scale)
    left_new = DECAY * left + (1.0 - DECAY) * jnp.einsum(
        "kij,klj->kil", summed, summed, precision=highest
    )
    right_new = DECAY * right + (1.0 - DECAY) * jnp.einsum(
        "kji,kjl->kil", summed, summed, precision=highest
    )
    half_way = jnp.einsum("kij,kjl->kil", left_root, summed, precision=highest)
    product = jnp.einsum("kij,kjl->kil", half_way, right_root, precision=highest)
    grad_power = jnp.sqrt(jnp.mean(summed * summed, axis=(1, 2)) + EPSILON)
    prod_power = jnp.sqrt(jnp.mean(product * product, axis=(1, 2)) + EPSILON)
    moved = (product * (grad_power / prod_power)[:, None, None]).astype(jnp.bfloat16)
    left_values, left_steps = requantize(left_new)
    right_values, right_steps = requantize(right_new)
    return (moved, left_values, left_steps, right_values, right_steps)


def local(
    grads,
    table,
    left_code,
    left_scale,
    right_code,
    right_scale,
    left_root_code,
    left_root_scale,
    right_root_code,
    right_root_scale,
):
    shards = lax.axis_size("shard")
    copies = lax.axis_size("replica")
    slot_count = left_code.shape[0]
    block_count = table.shape[0]
    own_grads = grads[0]
    picked = jnp.take(own_grads, table, axis=0)
    regrouped = lax.all_to_all(picked, "shard", split_axis=0, concat_axis=1, tiled=True)
    summed = lax.psum_scatter(
        regrouped.astype(jnp.float32).astype(jnp.bfloat16),
        "replica",
        scatter_dimension=0,
        tiled=True,
    ).astype(jnp.float32)
    moved, left_values, left_steps, right_values, right_steps = precondition(
        summed,
        left_code,
        left_scale,
        right_code,
        right_scale,
        left_root_code,
        left_root_scale,
        right_root_code,
        right_root_scale,
    )
    inverse = (
        jnp.zeros((block_count,), jnp.int32).at[table].set(jnp.arange(block_count, dtype=jnp.int32))
    )
    row_pieces = lax.all_to_all(moved, "shard", split_axis=1, concat_axis=0, tiled=True)
    spread = lax.all_gather(row_pieces, "replica", axis=0, tiled=True)
    placing = jnp.transpose(
        jnp.arange(block_count, dtype=jnp.int32).reshape(copies, shards, slot_count), (1, 0, 2)
    ).reshape(-1)
    direction = jnp.take(spread, jnp.take(placing, inverse, axis=0), axis=0)
    return (direction, left_values, left_steps, right_values, right_steps)


def solution(mesh):
    placed = (
        P("replica", None, "shard", None),
        P(),
        P(("shard", "replica"), None, None),
        P(("shard", "replica"), None, None),
        P(("shard", "replica"), None, None),
        P(("shard", "replica"), None, None),
        P(("shard", "replica"), None, None),
        P(("shard", "replica"), None, None),
        P(("shard", "replica"), None, None),
        P(("shard", "replica"), None, None),
    )
    return jax.shard_map(
        local,
        mesh=mesh,
        in_specs=placed,
        out_specs=(
            P(None, "shard", None),
            P(("shard", "replica"), None, None),
            P(("shard", "replica"), None, None),
            P(("shard", "replica"), None, None),
            P(("shard", "replica"), None, None),
        ),
        check_vma=False,
    )
```

profile of v0, /device:TPU:0, one launch (start us, length us, event | category | flops | bytes accessed | tf_op | source)
XLA Modules:
  0.0 87.3 jit_solution(14110696507606091491)
XLA Ops:
  7.2 0.7 compare_select_fusion.2
  8.0 0.3 copy-done
  8.2 0.6 gather_fusion.1
  9.0 14.7 %all_to_all.30 = bf16[32,32,256]{2,1,0:T(8,128)(2,1)S(1)} all-to-all(bf16[32,32,256]{2,1,0:T(8,128)(2,1)S(1)} %broadcast_select_fusion.1), channel_id=1, replica_groups=mesh['shard'=8,'replica'=4] {'shard'}, dimensions={0} | all-to-all | bytes 1048576 | tf_op jit(solution)/shard_map/all_to_all | solution.py:78
  23.7 0.8 copy.43
  24.5 0.7 copy-done.6
  25.3 0.3 mul.99
  25.9 0.5 copy-done.7
  26.5 0.3 mul.104
  27.1 0.6 copy-done.3
  27.8 0.8 copy-done.4
  28.8 0.7 scatter_custom_fusion
  29.5 0.7 gather_fusion
  30.2 15.5 %reduce-scatter.2.cloned.1.call-done = bf16[1,256,256]{2,1,0:T(8,128)(2,1)} async-done(((bf16[4,256,256]{2,1,0:T(8,128)(2,1)}), bf16[1,256,256]{2,1,0:T(8,128)(2,1)}) %reduce-scatter.2.cloned.1.call-update) | async-done | bytes 131088 | tf_op jit(solution)/shard_map/reduce_scatter | solution.py:79
  45.7 1.6 %multiply_reduce_fusion.1 = f32[]{:T(128)} fusion(bf16[1,256,256]{2,1,0:T(8,128)(2,1)} %reduce-scatter.2.cloned.1.call-done), kind=kLoop, calls=%fused_computation.26 | loop fusion | flops 196607 | bytes 131076 | tf_op jit(solution)/shard_map/reduce_sum | solution.py:52
  48.1 0.3 fusion.8
  48.3 0.6 copy-done.2
  49.0 1.0 %multiply_reduce_fusion = (f32[]{:T(128)}, f32[256,256]{1,0:T(8,128)S(1)}) fusion(f32[256,256]{1,0:T(8,128)S(1)} %fusion.8, f32[1,256,256]{2,1,0:T(8,128)S(1)} %mul.105, bf16[1,256,256]{2,1,0:T(8,128)(2,1)S(1)} %copy-done.2), kind=kOutput, calls=%fused_computation.25 | convolution fusion | flops 201588736 | bytes 917508 | tf_op jit(solution)/shard_map/kij,kjl->kil/dot_general | solution.py:51
  50.9 0.5 broadcast.161
  51.4 1.4 %reduce.7 = bf16[256,256]{1,0:T(8,128)(2,1)S(1)} reduce(bf16[256,1,256]{2,1,0:T(2,128)(2,1)S(1)} %bitcast.83, bf16[]{:T(256)} %broadcast.161), dimensions={1}, to_apply=%bitcast.77.reduce_sub_computation | reduce | bytes 262146
  52.8 0.7 reshape.310
  53.5 3.8 %all-to-all-start.1 = ((bf16[8,2,4096]{2,1,0:T(2,128)(2,1)}), bf16[8,2,4096]{2,1,0:T(2,128)(2,1)S(1)}, u32[]{:S(2)}, u32[]{:S(2)}) async-start(bf16[8,2,4096]{2,1,0:T(2,128)(2,1)} %reshape.310), calls=%async_computation.2 | async-start | bytes 262144 | tf_op jit(solution)/shard_map/all_to_all | solution.py:99
  57.3 0.2 bitcast_reduce_fusion.1
  57.6 0.4 copy-done.9
  58.0 0.2 bitcast_reduce_fusion
  58.3 0.6 fusion.20
  58.9 0.8 copy.48
  59.7 0.8 copy.49
  60.4 2.4 %all-to-all-done.1 = bf16[8,2,4096]{2,1,0:T(2,128)(2,1)S(1)} async-done(((bf16[8,2,4096]{2,1,0:T(2,128)(2,1)}), bf16[8,2,4096]{2,1,0:T(2,128)(2,1)S(1)}, u32[]{:S(2)}, u32[]{:S(2)}) %all-to-all-start.1) | async-done | bytes 131104 | tf_op jit(solution)/shard_map/all_to_all | solution.py:99
  63.0 16.0 %all_gather.3 = bf16[32,32,256]{2,1,0:T(8,128)(2,1)S(1)} all-gather(bf16[8,32,256]{2,1,0:T(8,128)(2,1)S(1)} %bitcast.85), channel_id=1, replica_groups=mesh['shard'=8,'replica'=4] {'replica'}, dimensions={0}, use_global_device_ids=true | all-gather | bytes 655360 | tf_op jit(solution)/shard_map/all_gather | solution.py:100
  78.9 0.6 gather_fusion.2
  79.5 0.9 %broadcast_select_fusion = bf16[32,32,256]{2,1,0:T(8,128)(2,1)} fusion(bf16[32,32,256]{2,1,0:T(8,128)(2,1)S(1)} %gather_fusion.2, pred[32]{0:T(512)(128)(4,1)S(1)} %get-tuple-element.31), kind=kLoop, calls=%fused_computation.8 | loop fusion | flops 262144 | bytes 1048608 | tf_op jit(solution)/shard_map/jit(_take)/select_n | solution.py:104
  (41 shorter events, 1.7 us)
Async XLA Ops:
  7.2 1.1 %copy-start = (bf16[1,32,32,256]{3,2,1,0:T(8,128)(2,1)S(1)}, bf16[1,32,32,256]{3,2,1,0:T(8,128)(2,1)}, u32[]{:S(2)}) copy-start(bf16[1,32,32,256]{3,2,1,0:T(8,128)(2,1)} %param.12) | copy-start | bytes 1572868
  7.2 0.8 copy-start.10
  7.2 38.5 %reduce-scatter.2.cloned.1.call-start = ((), (), s32[]{:S(2)}) async-start(), calls=%async_computation.3 | async-start | bytes 655360 | tf_op jit(solution)/shard_map/reduce_scatter | solution.py:79
  24.5 0.7 copy-start.6
  25.7 0.7 copy-start.7
  26.8 0.9 %copy-start.3 = (bf16[1,256,256]{2,1,0:T(8,128)(2,1)S(1)}, bf16[1,256,256]{2,1,0:T(8,128)(2,1)}, u32[]{:S(2)}) copy-start(bf16[1,256,256]{2,1,0:T(8,128)(2,1)} %param.14) | copy-start | bytes 393220
  27.7 0.9 %copy-start.4 = (bf16[1,256,256]{2,1,0:T(8,128)(2,1)S(1)}, bf16[1,256,256]{2,1,0:T(8,128)(2,1)}, u32[]{:S(2)}) copy-start(bf16[1,256,256]{2,1,0:T(8,128)(2,1)} %param.16) | copy-start | bytes 393220
  29.5 18.6 %copy-start.5 = (bf16[1,256,256]{2,1,0:T(8,128)(2,1)S(1)}, bf16[1,256,256]{2,1,0:T(8,128)(2,1)}, u32[]{:S(2)}) copy-start(bf16[1,256,256]{2,1,0:T(8,128)(2,1)} %param.18) | copy-start | bytes 393220
  45.7 2.4 %copy-start.1 = (bf16[1,256,256]{2,1,0:T(8,128)(2,1)S(1)}, bf16[1,256,256]{2,1,0:T(8,128)(2,1)}, u32[]{:S(2)}) copy-start(bf16[1,256,256]{2,1,0:T(8,128)(2,1)} %reduce-scatter.2.cloned.1.call-done) | copy-start | bytes 393220
  48.1 0.9 %copy-start.2 = (bf16[1,256,256]{2,1,0:T(8,128)(2,1)S(1)}, bf16[1,256,256]{2,1,0:T(8,128)(2,1)}, u32[]{:S(2)}) copy-start(bf16[1,256,256]{2,1,0:T(8,128)(2,1)} %param.20) | copy-start | bytes 393220
  53.5 3.8 %copy-start.8 = (f32[1,2,256]{2,1,0:T(2,128)S(1)}, f32[1,2,256]{2,1,0:T(2,128)}, u32[]{:S(2)}) copy-start(f32[1,2,256]{2,1,0:T(2,128)} %param.15) | copy-start | bytes 6148
  53.5 9.3 %all-to-all-start.1 = ((bf16[8,2,4096]{2,1,0:T(2,128)(2,1)}), bf16[8,2,4096]{2,1,0:T(2,128)(2,1)S(1)}, u32[]{:S(2)}, u32[]{:S(2)}) async-start(bf16[8,2,4096]{2,1,0:T(2,128)(2,1)} %reshape.310), calls=%async_computation.2 | async-start | bytes 262144 | tf_op jit(solution)/shard_map/all_to_all | solution.py:99
  57.3 0.7 copy-start.9
Sparse Core Ops, SparseCore 0:
  24.6 20.9 reduce-scatter.1
where the time goes:
time: 87.7 us; the launch traced here: 87.3 us
  blocking collectives  30.7 us (35%)
  waiting for transfers between devices  17.9 us (20%)
  between operations  15.7 us (18%)
  local copies, waits for them, and re-layouts  12 us (14%)
  other arithmetic  5.49 us (6%)
  starting transfers between devices  3.8 us (4%)
  matrix products  1.76 us (2%)
    all_gather x1, blocking collectives, local(): spread = lax.all_gather(row_pieces, 'replica', axis=0, tiled=True)  16 us
    reduce_scatter x1, waiting for transfers between devices, local(): lax.psum_scatter(regrouped.astype(jnp.float32).astype(jnp.bfloat16), 'rep...  15.5 us
    all_to_all x1, blocking collectives, local(): lax.all_to_all(picked, 'shard', split_axis=0, concat_axis=1, tiled=True)  14.7 us
    unnamed x30, local copies, waits for them, and re-layouts  6.92 us
    all_to_all x1, starting transfers between devices, local(): lax.all_to_all(moved, 'shard', split_axis=1, concat_axis=0, tiled=True)  3.76 us
    all_to_all x1, waiting for transfers between devices, local(): lax.all_to_all(moved, 'shard', split_axis=1, concat_axis=0, tiled=True)  2.37 us
  transfers between devices with their start and end apart: 2, of which 2 were waited for; matrix products, arithmetic and copies ran while one was open for 7% of the time, Pallas kernels for 0%

commit v1 on v0

v1 whole, which is shorter than its diff:
```python
import functools

import jax
import jax.numpy as jnp
from jax import lax
from jax.experimental import pallas as pl
from jax.experimental.pallas import tpu as pltpu
from jax.sharding import PartitionSpec as P

QG = 128
DECAY = 0.9
EPSILON = 1e-06
MESH = pl.DeviceIdType.MESH
F32 = jnp.float32
BF16 = jnp.bfloat16


def kernel(
    shards,
    copies,
    table,
    grads_hbm,
    lc_hbm,
    ls_hbm,
    rc_hbm,
    rs_hbm,
    lrc_hbm,
    lrs_hbm,
    rrc_hbm,
    rrs_hbm,
    direction,
    new_left,
    new_left_scale,
    new_right,
    new_right_scale,
    grads,
    lc,
    ls,
    rc,
    rs,
    lrc,
    lrs,
    rrc,
    rrs,
    packed,
    arrived,
    part,
    full,
    moved,
    got,
    place,
    in_sem,
    a1_send,
    a1_recv,
    a2_send,
    a2_recv,
    b1_send,
    b1_recv,
    b2_send,
    b2_recv,
):
    me_s = lax.axis_index("shard")
    me_r = lax.axis_index("replica")
    rows = grads.shape[1]
    order = lc.shape[1]
    blocks = shards * copies

    loads = []
    for k, (src, dst) in enumerate(
        [
            (grads_hbm.at[0], grads),
            (lrc_hbm, lrc),
            (lrs_hbm, lrs),
            (rrc_hbm, rrc),
            (rrs_hbm, rrs),
            (lc_hbm, lc),
            (ls_hbm, ls),
            (rc_hbm, rc),
            (rs_hbm, rs),
        ]
    ):
        copy = pltpu.make_async_copy(src, dst, in_sem.at[k])
        copy.start()
        loads.append(copy)

    barrier = pltpu.get_barrier_semaphore()
    for d in range(1, copies):
        pl.semaphore_signal(
            barrier, inc=1, device_id=(me_s, lax.rem(me_r + d, copies)), device_id_type=MESH
        )
    for d in range(1, shards):
        pl.semaphore_signal(
            barrier, inc=1, device_id=(lax.rem(me_s + d, shards), me_r), device_id_type=MESH
        )

    loads[0].wait()

    def pack(k, carry):
        packed[k] = grads[table[lax.rem(k, shards) * copies + k // shards]]
        return carry

    lax.fori_loop(0, blocks, pack, 0, unroll=4)
    pl.semaphore_wait(barrier, copies - 1 + shards - 1)

    sends = []
    for d in range(1, copies):
        to = lax.rem(me_r + d, copies)
        copy = pltpu.make_async_remote_copy(
            src_ref=packed.at[pl.ds(to * shards, shards)],
            dst_ref=arrived.at[d - 1],
            send_sem=a1_send.at[d - 1],
            recv_sem=a1_recv.at[d - 1],
            device_id=(me_s, to),
            device_id_type=MESH,
        )
        copy.start()
        sends.append(copy)

    def locate(b, carry):
        def look(q, found):
            spot = lax.rem(q, copies) * shards + q // copies
            return jnp.where(table[q] == b, spot, found)

        place[b] = lax.fori_loop(0, blocks, look, jnp.int32(0), unroll=8)
        return carry

    lax.fori_loop(0, blocks, locate, 0)

    for copy in sends:
        copy.wait()
    total = packed[pl.ds(me_r * shards, shards)].astype(F32)
    for d in range(1, copies):
        total = total + arrived[d - 1].astype(F32)
    part[...] = total.astype(BF16)

    sends = []
    for d in range(1, shards):
        to = lax.rem(me_s + d, shards)
        copy = pltpu.make_async_remote_copy(
            src_ref=part.at[to],
            dst_ref=full.at[me_s],
            send_sem=a2_send.at[d - 1],
            recv_sem=a2_recv.at[d - 1],
            device_id=(to, me_r),
            device_id_type=MESH,
        )
        copy.start()
        sends.append(copy)
    full[me_s] = part[me_s]
    for copy in loads[1:]:
        copy.wait()
    zeros = jnp.zeros((2, order), F32)
    columns = jnp.concatenate([ls[0], rs[0], lrs[0], zeros], axis=0).T
    for copy in sends:
        copy.wait()

    summed32 = full[...].astype(F32).reshape(order, order)
    summed = summed32.astype(BF16)
    half = columns[:, 4:5] * jnp.dot(lrc[0, :, :QG], summed[:QG], preferred_element_type=F32)
    half = half + columns[:, 5:6] * jnp.dot(
        lrc[0, :, QG:], summed[QG:], preferred_element_type=F32
    )
    product = jnp.concatenate(
        [
            jnp.dot(
                (half * rrs[0, g : g + 1]).astype(BF16),
                rrc[0, :, g * QG : (g + 1) * QG],
                preferred_element_type=F32,
            )
            for g in range(order // QG)
        ],
        axis=1,
    )
    count = 1.0 / (order * order)
    grad_power = jnp.sum(jnp.sum(summed32 * summed32, axis=0, keepdims=True), axis=1, keepdims=True)
    prod_power = jnp.sum(jnp.sum(product * product, axis=0, keepdims=True), axis=1, keepdims=True)
    ratio = jnp.sqrt(grad_power * count + EPSILON) / jnp.sqrt(prod_power * count + EPSILON)
    moved[...] = (product * ratio).reshape(shards, rows, order).astype(BF16)

    mine = me_r * shards
    sends = []
    for d in range(1, shards):
        to = lax.rem(me_s + d, shards)
        copy = pltpu.make_async_remote_copy(
            src_ref=moved.at[to],
            dst_ref=got.at[mine + me_s],
            send_sem=b1_send.at[d - 1],
            recv_sem=b1_recv.at[d - 1],
            device_id=(to, me_r),
            device_id_type=MESH,
        )
        copy.start()
        sends.append(copy)
    got[mine + me_s] = moved[me_s]
    for copy in sends:
        copy.wait()

    sends = []
    for d in range(1, copies):
        to = lax.rem(me_r + d, copies)
        copy = pltpu.make_async_remote_copy(
            src_ref=got.at[pl.ds(mine, shards)],
            dst_ref=got.at[pl.ds(mine, shards)],
            send_sem=b2_send.at[d - 1],
            recv_sem=b2_recv.at[d - 1],
            device_id=(me_s, to),
            device_id_type=MESH,
        )
        copy.start()
        sends.append(copy)

    scales = []
    lane = lax.broadcasted_iota(jnp.int32, (order, QG), 1)
    table_of_scales = jnp.zeros((order, QG), F32)
    for k, (code, gram, out) in enumerate(
        [
            (
                lc,
                lax.dot_general(
                    summed, summed, (((1,), (1,)), ((), ())), preferred_element_type=F32
                ),
                new_left,
            ),
            (
                rc,
                lax.dot_general(
                    summed, summed, (((0,), (0,)), ((), ())), preferred_element_type=F32
                ),
                new_right,
            ),
        ]
    ):
        for g in range(order // QG):
            at = 2 * k + g
            cols = slice(g * QG, (g + 1) * QG)
            old = code[0, :, cols].astype(F32) * columns[:, at : at + 1]
            new = DECAY * old + (1.0 - DECAY) * gram[:, cols]
            step = (jnp.max(jnp.abs(new), axis=1, keepdims=True) + EPSILON) / 7.0
            out[0, :, cols] = (new * (1.0 / step)).astype(BF16)
            table_of_scales = jnp.where(lane == at, step, table_of_scales)
    flipped = table_of_scales.T
    new_left_scale[0] = flipped[0:2]
    new_right_scale[0] = flipped[2:4]

    for copy in sends:
        copy.wait()

    def put(b, carry):
        direction[b] = got[place[b]]
        return carry

    lax.fori_loop(0, blocks, put, 0, unroll=4)


def local(shards, copies, grads, table, *factors):
    blocks, rows, order = grads.shape[1:]
    vmem = pl.BlockSpec(memory_space=pltpu.VMEM)
    hbm = pl.BlockSpec(memory_space=pl.ANY)
    code = jax.ShapeDtypeStruct((1, order, order), BF16)
    scale = jax.ShapeDtypeStruct((1, order // QG, order), F32)
    dma = pltpu.SemaphoreType.DMA
    return pl.pallas_call(
        functools.partial(kernel, shards, copies),
        out_shape=[jax.ShapeDtypeStruct((blocks, rows, order), BF16), code, scale, code, scale],
        in_specs=[pl.BlockSpec(memory_space=pltpu.SMEM)] + [hbm] * 9,
        out_specs=[vmem] * 5,
        scratch_shapes=[pltpu.VMEM((blocks, rows, order), BF16)]
        + [pltpu.VMEM(f.shape, f.dtype) for f in factors]
        + [
            pltpu.VMEM((blocks, rows, order), BF16),
            pltpu.VMEM((copies - 1, shards, rows, order), BF16),
            pltpu.VMEM((shards, rows, order), BF16),
            pltpu.VMEM((shards, rows, order), BF16),
            pltpu.VMEM((shards, rows, order), BF16),
            pltpu.VMEM((blocks, rows, order), BF16),
            pltpu.SMEM((blocks,), jnp.int32),
            dma((9,)),
            dma((copies - 1,)),
            dma((copies - 1,)),
            dma((shards - 1,)),
            dma((shards - 1,)),
            dma((shards - 1,)),
            dma((shards - 1,)),
            dma((copies - 1,)),
            dma((copies - 1,)),
        ],
        compiler_params=pltpu.CompilerParams(
            collective_id=0, has_side_effects=True, vmem_limit_bytes=48 * 1024 * 1024
        ),
    )(table, grads, *factors)


def solution(mesh):
    slots = P(("shard", "replica"), None, None)
    return jax.shard_map(
        functools.partial(local, mesh.shape["shard"], mesh.shape["replica"]),
        mesh=mesh,
        in_specs=(P("replica", None, "shard", None), P()) + (slots,) * 8,
        out_specs=(P(None, "shard", None), slots, slots, slots, slots),
        check_vma=False,
    )
```

time: 87.7 us -> 50.3 us (0.57)
  Pallas kernels: 0 us -> 37.5 us
  blocking collectives: 30.7 us -> 0 us
  waiting for transfers between devices: 17.9 us -> 0 us
  between operations: 15.7 us -> 0.66 us
  other arithmetic: 5.49 us -> 0 us
  starting transfers between devices: 3.8 us -> 0 us
  matrix products: 1.76 us -> 0 us
    pallas_call x0 -> x1, Pallas kernels: none -> 37.5 us  [local(): pl.pallas_call(functools.partial(kernel, shards, copies), out_shape=[jax....]
    all_gather x1 -> x0, blocking collectives: 16 us -> none  [local(): spread = lax.all_gather(row_pieces, 'replica', axis=0, tiled=True)]
    reduce_scatter x1 -> x0, waiting for transfers between devices: 15.5 us -> none  [local(): lax.psum_scatter(regrouped.astype(jnp.float32).astype(jnp.bfloat16), 'rep...]
    all_to_all x1 -> x0, blocking collectives: 14.7 us -> none  [local(): lax.all_to_all(picked, 'shard', split_axis=0, concat_axis=1, tiled=True)]
    unnamed x30 -> x25, local copies, waits for them, and re-layouts: 6.92 us -> 11.3 us
    all_to_all x1 -> x0, starting transfers between devices: 3.76 us -> none  [local(): lax.all_to_all(moved, 'shard', split_axis=1, concat_axis=0, tiled=True)]
    all_to_all x1 -> x0, waiting for transfers between devices: 2.37 us -> none  [local(): lax.all_to_all(moved, 'shard', split_axis=1, concat_axis=0, tiled=True)]
    gather x3 -> x0, local copies, waits for them, and re-layouts: 1.86 us -> none  [the longest x2 1.28 us: local(): direction = jnp.take(spread, jnp.take(placing, inverse, axis=0), axis=0)]
  transfers between devices with their start and end apart: 2 -> 0, of which waited for: 2 -> 0; matrix products, arithmetic and copies ran while one was open for 7% -> 0% of each run, Pallas kernels for 0% -> 0%
where the time goes in v1:
time: 50.3 us; the launch traced here: 49.5 us
  Pallas kernels  37.5 us (75%)
  local copies, waits for them, and re-layouts  11.3 us (22%)
  between operations  0.66 us (1%)
    pallas_call x1, Pallas kernels, local(): pl.pallas_call(functools.partial(kernel, shards, copies), out_shape=[jax....  37.5 us
    unnamed x25, local copies, waits for them, and re-layouts  11.3 us

profile of v1, /device:TPU:0, one launch (start us, length us, event | category | flops | bytes accessed | tf_op | source)
XLA Modules:
  0.0 49.5 jit_solution(5299217110345439638)
XLA Ops:
  0.6 0.0 copy-start
  0.6 1.0 %copy-done = bf16[1,32,32,256]{3,2,1,0:T(8,128)(2,1)S(1)} copy-done((bf16[1,32,32,256]{3,2,1,0:T(8,128)(2,1)S(1)}, bf16[1,32,32,256]{3,2,1,0:T(8,128)(2,1)}, u32[]{:S(2)}) %copy-start) | copy-done | bytes 524312
  1.7 0.0 copy-start.1
  1.7 0.9 %copy-done.1 = bf16[1,256,256]{2,1,0:T(8,128)(2,1)S(1)} copy-done((bf16[1,256,256]{2,1,0:T(8,128)(2,1)S(1)}, bf16[1,256,256]{2,1,0:T(8,128)(2,1)}, u32[]{:S(2)}) %copy-start.1) | copy-done | bytes 131096
  2.6 0.0 copy-start.2
  2.6 0.9 %copy-done.2 = bf16[1,256,256]{2,1,0:T(8,128)(2,1)S(1)} copy-done((bf16[1,256,256]{2,1,0:T(8,128)(2,1)S(1)}, bf16[1,256,256]{2,1,0:T(8,128)(2,1)}, u32[]{:S(2)}) %copy-start.2) | copy-done | bytes 131096
  3.5 0.0 copy-start.3
  3.5 0.9 %copy-done.3 = bf16[1,256,256]{2,1,0:T(8,128)(2,1)S(1)} copy-done((bf16[1,256,256]{2,1,0:T(8,128)(2,1)S(1)}, bf16[1,256,256]{2,1,0:T(8,128)(2,1)}, u32[]{:S(2)}) %copy-start.3) | copy-done | bytes 131096
  4.4 0.0 copy-start.4
  4.4 0.9 %copy-done.4 = bf16[1,256,256]{2,1,0:T(8,128)(2,1)S(1)} copy-done((bf16[1,256,256]{2,1,0:T(8,128)(2,1)S(1)}, bf16[1,256,256]{2,1,0:T(8,128)(2,1)}, u32[]{:S(2)}) %copy-start.4) | copy-done | bytes 131096
  5.3 0.0 copy-start.5
  5.3 0.7 %copy-done.5 = f32[1,2,256]{2,1,0:T(2,128)S(1)} copy-done((f32[1,2,256]{2,1,0:T(2,128)S(1)}, f32[1,2,256]{2,1,0:T(2,128)}, u32[]{:S(2)}) %copy-start.5) | copy-done | bytes 2072
  6.0 0.0 copy-start.6
  6.0 0.7 %copy-done.6 = f32[1,2,256]{2,1,0:T(2,128)S(1)} copy-done((f32[1,2,256]{2,1,0:T(2,128)S(1)}, f32[1,2,256]{2,1,0:T(2,128)}, u32[]{:S(2)}) %copy-start.6) | copy-done | bytes 2072
  6.7 0.0 copy-start.7
  6.7 0.7 %copy-done.7 = f32[1,2,256]{2,1,0:T(2,128)S(1)} copy-done((f32[1,2,256]{2,1,0:T(2,128)S(1)}, f32[1,2,256]{2,1,0:T(2,128)}, u32[]{:S(2)}) %copy-start.7) | copy-done | bytes 2072
  7.3 0.0 copy-start.8
  7.3 0.7 %copy-done.8 = f32[1,2,256]{2,1,0:T(2,128)S(1)} copy-done((f32[1,2,256]{2,1,0:T(2,128)S(1)}, f32[1,2,256]{2,1,0:T(2,128)}, u32[]{:S(2)}) %copy-start.8) | copy-done | bytes 2072
  8.0 0.0 copy-start.9
  8.0 0.7 %copy-done.9 = s32[32]{0:T(128)S(1)} copy-done((s32[32]{0:T(128)S(1)}, s32[32]{0:T(128)}, u32[]{:S(2)}) %copy-start.9) | copy-done | bytes 152
  8.7 37.5 %shard_map.137 = (bf16[32,32,256]{2,1,0:T(8,128)(2,1)S(1)}, bf16[1,256,256]{2,1,0:T(8,128)(2,1)S(1)}, f32[1,2,256]{2,1,0:T(2,128)S(1)}, bf16[1,256,256]{2,1,0:T(8,128)(2,1)S(1)}, f32[1,2,256]{2,1,0:T(2,128)S(1)}) custom-call(s32[32]{0:T(128)S(1)} %copy-done.9, bf16[1,32,32,256]{3,2,1,0:T(8,128)(2,1)S(1)} %copy-done, bf16[1,256,256]{2,1,0:T(8,128)(2,1)S(1)} %copy-done.1, ...), custom_call_target="tpu_custom_call" | custom-call | tf_op jit(solution)/shard_map/pallas_call | solution.py:262
  46.2 0.8 %copy.20 = bf16[32,32,256]{2,1,0:T(8,128)(2,1)} copy(bf16[32,32,256]{2,1,0:T(8,128)(2,1)S(1)} %get-tuple-element.10) | data formatting | bytes 1048576
  47.0 0.7 %copy.21 = bf16[1,256,256]{2,1,0:T(8,128)(2,1)} copy(bf16[1,256,256]{2,1,0:T(8,128)(2,1)S(1)} %get-tuple-element.11) | data formatting | bytes 262144
  47.7 0.6 %copy.22 = f32[1,2,256]{2,1,0:T(2,128)} copy(f32[1,2,256]{2,1,0:T(2,128)S(1)} %get-tuple-element.12) | data formatting | bytes 4096
  48.2 0.7 %copy.23 = bf16[1,256,256]{2,1,0:T(8,128)(2,1)} copy(bf16[1,256,256]{2,1,0:T(8,128)(2,1)S(1)} %get-tuple-element.13) | data formatting | bytes 262144
  48.9 0.6 %copy.24 = f32[1,2,256]{2,1,0:T(2,128)} copy(f32[1,2,256]{2,1,0:T(2,128)S(1)} %get-tuple-element.14) | data formatting | bytes 4096
Async XLA Ops:
  0.6 1.0 %copy-start = (bf16[1,32,32,256]{3,2,1,0:T(8,128)(2,1)S(1)}, bf16[1,32,32,256]{3,2,1,0:T(8,128)(2,1)}, u32[]{:S(2)}) copy-start(bf16[1,32,32,256]{3,2,1,0:T(8,128)(2,1)} %grads_hbm.1) | copy-start | bytes 1572868
  1.7 0.9 %copy-start.1 = (bf16[1,256,256]{2,1,0:T(8,128)(2,1)S(1)}, bf16[1,256,256]{2,1,0:T(8,128)(2,1)}, u32[]{:S(2)}) copy-start(bf16[1,256,256]{2,1,0:T(8,128)(2,1)} %lc_hbm.1) | copy-start | bytes 393220
  2.6 0.9 %copy-start.2 = (bf16[1,256,256]{2,1,0:T(8,128)(2,1)S(1)}, bf16[1,256,256]{2,1,0:T(8,128)(2,1)}, u32[]{:S(2)}) copy-start(bf16[1,256,256]{2,1,0:T(8,128)(2,1)} %rc_hbm.1) | copy-start | bytes 393220
  3.5 0.9 %copy-start.3 = (bf16[1,256,256]{2,1,0:T(8,128)(2,1)S(1)}, bf16[1,256,256]{2,1,0:T(8,128)(2,1)}, u32[]{:S(2)}) copy-start(bf16[1,256,256]{2,1,0:T(8,128)(2,1)} %lrc_hbm.1) | copy-start | bytes 393220
  4.4 0.9 %copy-start.4 = (bf16[1,256,256]{2,1,0:T(8,128)(2,1)S(1)}, bf16[1,256,256]{2,1,0:T(8,128)(2,1)}, u32[]{:S(2)}) copy-start(bf16[1,256,256]{2,1,0:T(8,128)(2,1)} %rrc_hbm.1) | copy-start | bytes 393220
  5.3 0.7 %copy-start.5 = (f32[1,2,256]{2,1,0:T(2,128)S(1)}, f32[1,2,256]{2,1,0:T(2,128)}, u32[]{:S(2)}) copy-start(f32[1,2,256]{2,1,0:T(2,128)} %ls_hbm.1) | copy-start | bytes 6148
  6.0 0.7 %copy-start.6 = (f32[1,2,256]{2,1,0:T(2,128)S(1)}, f32[1,2,256]{2,1,0:T(2,128)}, u32[]{:S(2)}) copy-start(f32[1,2,256]{2,1,0:T(2,128)} %rs_hbm.1) | copy-start | bytes 6148
  6.7 0.7 %copy-start.7 = (f32[1,2,256]{2,1,0:T(2,128)S(1)}, f32[1,2,256]{2,1,0:T(2,128)}, u32[]{:S(2)}) copy-start(f32[1,2,256]{2,1,0:T(2,128)} %lrs_hbm.1) | copy-start | bytes 6148
  7.3 0.7 %copy-start.8 = (f32[1,2,256]{2,1,0:T(2,128)S(1)}, f32[1,2,256]{2,1,0:T(2,128)}, u32[]{:S(2)}) copy-start(f32[1,2,256]{2,1,0:T(2,128)} %rrs_hbm.1) | copy-start | bytes 6148
  8.0 0.7 %copy-start.9 = (s32[32]{0:T(128)S(1)}, s32[32]{0:T(128)}, u32[]{:S(2)}) copy-start(s32[32]{0:T(128)} %table.1) | copy-start | bytes 388

commit v2 on v1

v2 whole, which is shorter than its diff:
```python
import functools

import jax
import jax.numpy as jnp
from jax import lax
from jax.experimental import pallas as pl
from jax.experimental.pallas import tpu as pltpu
from jax.sharding import PartitionSpec as P

QG = 128
DECAY = 0.9
EPSILON = 1e-06
VMEM_BYTES = 64 * 1024 * 1024
MESH = pl.DeviceIdType.MESH
F32 = jnp.float32
BF16 = jnp.bfloat16


def kernel(
    shards,
    copies,
    cuts,
    table,
    grads_hbm,
    lc_hbm,
    ls_hbm,
    rc_hbm,
    rs_hbm,
    lrc_hbm,
    lrs_hbm,
    rrc_hbm,
    rrs_hbm,
    got,
    new_left,
    new_left_scale,
    new_right,
    new_right_scale,
    grads,
    lc,
    ls,
    rc,
    rs,
    lrc,
    lrs,
    rrc,
    rrs,
    packed,
    arrived,
    part,
    full,
    moved,
    in_sem,
    a1_send,
    a1_recv,
    a2_send,
    a2_recv,
    b1_send,
    b1_recv,
    b2_send,
    b2_recv,
):
    me_s = lax.axis_index("shard")
    me_r = lax.axis_index("replica")
    rows = grads.shape[1]
    order = lc.shape[1]
    blocks = shards * copies
    size = shards // cuts
    in_line = copies == 4

    loads = []
    for k, (src, dst) in enumerate(
        [
            (grads_hbm.at[0], grads),
            (lrc_hbm, lrc),
            (lrs_hbm, lrs),
            (rrc_hbm, rrc),
            (rrs_hbm, rrs),
            (lc_hbm, lc),
            (ls_hbm, ls),
            (rc_hbm, rc),
            (rs_hbm, rs),
        ]
    ):
        copy = pltpu.make_async_copy(src, dst, in_sem.at[k])
        copy.start()
        loads.append(copy)

    barrier = pltpu.get_barrier_semaphore()
    for d in range(1, copies):
        pl.semaphore_signal(
            barrier, inc=1, device_id=(me_s, lax.rem(me_r + d, copies)), device_id_type=MESH
        )
    for d in range(1, shards):
        pl.semaphore_signal(
            barrier, inc=1, device_id=(lax.rem(me_s + d, shards), me_r), device_id_type=MESH
        )

    loads[0].wait()

    def pack(k, carry):
        packed[k] = grads[table[lax.rem(k, shards) * copies + k // shards]]
        return carry

    lax.fori_loop(0, blocks, pack, 0, unroll=8)
    pl.semaphore_wait(barrier, copies - 1 + shards - 1)

    def group(r, c):
        return pl.ds(r * shards + c * size, size)

    def chunk(c):
        return pl.ds(c * size, size)

    partner = me_r + 1 - 2 * lax.rem(me_r, 2)
    opposite = copies - 1 - me_r
    across = copies - 1 - partner
    is_end = jnp.logical_or(me_r == 0, me_r == copies - 1)
    is_mid = jnp.logical_not(is_end)
    DIRECT, PAIR, RELAY = 0, 1, 2

    def a_copy(src, slot, c, k, to):
        return pltpu.make_async_remote_copy(
            src_ref=src,
            dst_ref=arrived.at[slot, chunk(c)],
            send_sem=a1_send.at[k, c],
            recv_sem=a1_recv.at[slot, c],
            device_id=(me_s, to),
            device_id_type=MESH,
        )

    def end_a(k, c):
        to_group = [across, partner, opposite][k]
        slot = [RELAY, DIRECT, RELAY + 1][k]
        return a_copy(packed.at[group(to_group, c)], slot, c, k, partner)

    def mid_direct(c):
        return a_copy(packed.at[group(partner, c)], DIRECT, c, 0, partner)

    def mid_relay(k, c):
        src = arrived.at[RELAY + k, chunk(c)]
        return a_copy(src, PAIR, c, 1 + k, [opposite, across][k])

    def relay(k):
        for c in range(cuts):
            a_copy(packed.at[chunk(c)], RELAY + k, c, 0, partner).wait_recv()
            own = packed[group([opposite, across][k], c)].astype(F32)
            arrived[RELAY + k, chunk(c)] = (
                arrived[RELAY + k, chunk(c)].astype(F32) + own
            ).astype(BF16)
            mid_relay(k, c).start()

    def far(d, c):
        to = lax.rem(me_r + d, copies)
        return a_copy(packed.at[group(to, c)], d - 1, c, d - 1, to)

    if in_line:

        @pl.when(is_end)
        def _():
            for k in range(3):
                for c in range(cuts):
                    end_a(k, c).start()

        @pl.when(is_mid)
        def _():
            for c in range(cuts):
                mid_direct(c).start()
            relay(0)

    else:
        for c in range(cuts):
            for d in range(1, copies):
                far(d, c).start()

    def a2_copy(to):
        return pltpu.make_async_remote_copy(
            src_ref=part.at[to],
            dst_ref=full.at[me_s],
            send_sem=a2_send.at[to],
            recv_sem=a2_recv.at[me_s],
            device_id=(to, me_r),
            device_id_type=MESH,
        )

    def a2_arrival(source):
        return pltpu.make_async_remote_copy(
            src_ref=part.at[source],
            dst_ref=full.at[source],
            send_sem=a2_send.at[source],
            recv_sem=a2_recv.at[source],
            device_id=(source, me_r),
            device_id_type=MESH,
        )

    for c in range(cuts):
        total = packed[group(me_r, c)].astype(F32)
        for slot in [DIRECT, PAIR] if in_line else range(copies - 1):
            a_copy(packed.at[chunk(c)], slot, c, 0, partner).wait_recv()
            total = total + arrived[slot, chunk(c)].astype(F32)
        part[chunk(c)] = total.astype(BF16)
        for k in range(size):
            to = c * size + lax.rem(me_s + k, size)

            @pl.when(to != me_s)
            def _():
                a2_copy(to).start()

    if in_line:

        @pl.when(is_mid)
        def _():
            relay(1)

    full[me_s] = part[me_s]
    for copy in loads[1:]:
        copy.wait()
    zeros = jnp.zeros((2, order), F32)
    columns = jnp.concatenate([ls[0], rs[0], lrs[0], zeros], axis=0).T
    for d in range(1, shards):
        a2_arrival(lax.rem(me_s + d, shards)).wait_recv()

    summed32 = full[...].astype(F32).reshape(order, order)
    summed = summed32.astype(BF16)
    half = columns[:, 4:5] * jnp.dot(lrc[0, :, :QG], summed[:QG], preferred_element_type=F32)
    half = half + columns[:, 5:6] * jnp.dot(
        lrc[0, :, QG:], summed[QG:], preferred_element_type=F32
    )
    product = jnp.concatenate(
        [
            jnp.dot(
                (half * rrs[0, g : g + 1]).astype(BF16),
                rrc[0, :, g * QG : (g + 1) * QG],
                preferred_element_type=F32,
            )
            for g in range(order // QG)
        ],
        axis=1,
    )
    count = 1.0 / (order * order)
    grad_power = jnp.sum(jnp.sum(summed32 * summed32, axis=0, keepdims=True), axis=1, keepdims=True)
    prod_power = jnp.sum(jnp.sum(product * product, axis=0, keepdims=True), axis=1, keepdims=True)
    ratio = jnp.sqrt(grad_power * count + EPSILON) / jnp.sqrt(prod_power * count + EPSILON)
    moved[...] = (product * ratio).reshape(shards, rows, order).astype(BF16)

    mine = me_r * shards

    def b1_copy(to):
        return pltpu.make_async_remote_copy(
            src_ref=moved.at[to],
            dst_ref=got.at[mine + me_s],
            send_sem=b1_send.at[to],
            recv_sem=b1_recv.at[me_s],
            device_id=(to, me_r),
            device_id_type=MESH,
        )

    def b1_arrival(source):
        return pltpu.make_async_remote_copy(
            src_ref=moved.at[source],
            dst_ref=got.at[mine + source],
            send_sem=b1_send.at[source],
            recv_sem=b1_recv.at[source],
            device_id=(source, me_r),
            device_id_type=MESH,
        )

    for d in range(1, shards):
        b1_copy(lax.rem(me_s + d, shards)).start()
    got[mine + me_s] = moved[me_s]

    lane = lax.broadcasted_iota(jnp.int32, (order, QG), 1)

    def statistic(k, code, contracted, out, steps):
        gram = lax.dot_general(
            summed, summed, (((contracted,), (contracted,)), ((), ())), preferred_element_type=F32
        )
        for g in range(order // QG):
            at = 2 * k + g
            cols = slice(g * QG, (g + 1) * QG)
            old = code[0, :, cols].astype(F32) * columns[:, at : at + 1]
            new = DECAY * old + (1.0 - DECAY) * gram[:, cols]
            step = (jnp.max(jnp.abs(new), axis=1, keepdims=True) + EPSILON) / 7.0
            out[0, :, cols] = (new * (1.0 / step)).astype(BF16)
            steps = jnp.where(lane == at, step, steps)
        return steps

    steps = statistic(0, lc, 1, new_left, jnp.zeros((order, QG), F32))

    def b_copy(r, c, k, to):
        return pltpu.make_async_remote_copy(
            src_ref=got.at[group(r, c)],
            dst_ref=got.at[group(r, c)],
            send_sem=b2_send.at[k, c],
            recv_sem=b2_recv.at[r, c],
            device_id=(me_s, to),
            device_id_type=MESH,
        )

    def own_sends(c):
        if not in_line:
            return [
                b_copy(me_r, c, d - 1, lax.rem(me_r + d, copies)) for d in range(1, copies)
            ]
        return [
            b_copy(me_r, c, 0, partner),
            b_copy(me_r, c, 1, jnp.where(is_end, across, opposite)),
        ]

    for c in range(cuts):
        for s in range(c * size, (c + 1) * size):

            @pl.when(s != me_s)
            def _():
                b1_arrival(s).wait_recv()

        for copy in own_sends(c):
            copy.start()

    steps = statistic(1, rc, 0, new_right, steps)
    flipped = steps.T
    new_left_scale[0] = flipped[0:2]
    new_right_scale[0] = flipped[2:4]

    if in_line:

        @pl.when(is_mid)
        def _():
            for k, r in enumerate([opposite, across]):
                for c in range(cuts):
                    b_copy(r, c, 2 + k, partner).wait_recv()
                    b_copy(r, c, 2 + k, partner).start()
            for c in range(cuts):
                b_copy(partner, c, 0, partner).wait_recv()
            for c in range(cuts):
                mid_direct(c).wait_send()
                for k in range(2):
                    mid_relay(k, c).wait_send()
                    b_copy([opposite, across][k], c, 2 + k, partner).wait_send()

        @pl.when(is_end)
        def _():
            for r in [partner, across, opposite]:
                for c in range(cuts):
                    b_copy(r, c, 0, partner).wait_recv()
            for c in range(cuts):
                for k in range(3):
                    end_a(k, c).wait_send()

    else:
        for c in range(cuts):
            for d in range(1, copies):
                b_copy(lax.rem(me_r + d, copies), c, 0, partner).wait_recv()
                far(d, c).wait_send()
    for c in range(cuts):
        for copy in own_sends(c):
            copy.wait_send()
    for d in range(1, shards):
        to = lax.rem(me_s + d, shards)
        a2_copy(to).wait_send()
        b1_copy(to).wait_send()


def place(shards, copies, table, got, *refs):
    stats, direction, outs, sem = refs[:4], refs[4], refs[5:9], refs[9]
    others = [
        pltpu.make_async_copy(src, dst, sem.at[1 + k])
        for k, (src, dst) in enumerate(zip(stats, outs))
    ]
    for copy in others:
        copy.start()

    def put(k, carry):
        block = table[lax.rem(k, shards) * copies + k // shards]
        pltpu.make_async_copy(got.at[k], direction.at[block], sem.at[0]).start()
        return carry

    lax.fori_loop(0, shards * copies, put, 0, unroll=8)
    pltpu.make_async_copy(got, direction, sem.at[0]).wait()
    for copy in others:
        copy.wait()


def local(shards, copies, grads, table, *factors):
    blocks, rows, order = grads.shape[1:]
    cuts = 2
    vmem = pl.BlockSpec(memory_space=pltpu.VMEM)
    smem = pl.BlockSpec(memory_space=pltpu.SMEM)
    hbm = pl.BlockSpec(memory_space=pltpu.HBM)
    code = jax.ShapeDtypeStruct((1, order, order), BF16)
    scale = jax.ShapeDtypeStruct((1, order // QG, order), F32)
    outs = [jax.ShapeDtypeStruct((blocks, rows, order), BF16), code, scale, code, scale]
    dma = pltpu.SemaphoreType.DMA
    results = pl.pallas_call(
        functools.partial(kernel, shards, copies, cuts),
        out_shape=outs,
        in_specs=[smem] + [hbm] * 9,
        out_specs=[vmem] * 5,
        scratch_shapes=[pltpu.VMEM((blocks, rows, order), BF16)]
        + [pltpu.VMEM(f.shape, f.dtype) for f in factors]
        + [
            pltpu.VMEM((blocks, rows, order), BF16),
            pltpu.VMEM((max(4, copies - 1), shards, rows, order), BF16),
            pltpu.VMEM((shards, rows, order), BF16),
            pltpu.VMEM((shards, rows, order), BF16),
            pltpu.VMEM((shards, rows, order), BF16),
            dma((9,)),
            dma((copies, cuts)),
            dma((copies, cuts)),
            dma((shards,)),
            dma((shards,)),
            dma((shards,)),
            dma((shards,)),
            dma((copies, cuts)),
            dma((copies, cuts)),
        ],
        compiler_params=pltpu.CompilerParams(
            collective_id=0, has_side_effects=True, vmem_limit_bytes=VMEM_BYTES
        ),
    )(table, grads, *factors)
    return pl.pallas_call(
        functools.partial(place, shards, copies),
        out_shape=outs,
        in_specs=[smem] + [hbm] * 5,
        out_specs=[hbm] * 5,
        scratch_shapes=[dma((5,))],
        compiler_params=pltpu.CompilerParams(vmem_limit_bytes=VMEM_BYTES),
    )(table, *results)


def solution(mesh):
    slots = P(("shard", "replica"), None, None)
    return jax.shard_map(
        functools.partial(local, mesh.shape["shard"], mesh.shape["replica"]),
        mesh=mesh,
        in_specs=(P("replica", None, "shard", None), P()) + (slots,) * 8,
        out_specs=(P(None, "shard", None), slots, slots, slots, slots),
        check_vma=False,
    )
```

time: 50.3 us -> 66 us (1.31)
  Pallas kernels: 37.5 us -> 65.2 us
  local copies, waits for them, and re-layouts: 11.3 us -> 0 us
    pallas_call x1 -> x2, Pallas kernels: 37.5 us -> 65.2 us  [the longest x1 39.4 us: local(): pl.pallas_call(functools.partial(kernel, shards, copies, cuts), out_shape...]
    unnamed x25 -> x0, local copies, waits for them, and re-layouts: 11.3 us -> none
where the time goes in v2:
time: 66 us; the launch traced here: 65.8 us
  Pallas kernels  65.2 us (99%)
    pallas_call x1, Pallas kernels, local(): pl.pallas_call(functools.partial(kernel, shards, copies, cuts), out_shape...  39.4 us
    pallas_call x1, Pallas kernels, local(): pl.pallas_call(functools.partial(place, shards, copies), out_shape=outs,...  25.8 us

profile of v2, /device:TPU:0, one launch (start us, length us, event | category | flops | bytes accessed | tf_op | source)
XLA Modules:
  0.0 65.8 jit_solution(9602407975406590164)
XLA Ops:
  0.6 39.4 %shard_map.137 = (bf16[32,32,256]{2,1,0:T(8,128)(2,1)}, bf16[1,256,256]{2,1,0:T(8,128)(2,1)}, f32[1,2,256]{2,1,0:T(2,128)}, bf16[1,256,256]{2,1,0:T(8,128)(2,1)}, f32[1,2,256]{2,1,0:T(2,128)}) custom-call(s32[32]{0:T(128)} %table.3, bf16[1,32,32,256]{3,2,1,0:T(8,128)(2,1)} %grads_hbm.1, bf16[1,256,256]{2,1,0:T(8,128)(2,1)} %lc_hbm.1, f32[1,2,256]{2,1,0:T(2,128)} %ls_hbm.1, ...), custom_call_target="tpu_custom_call" | custom-call | tf_op jit(solution)/shard_map/pallas_call | solution.py:392
  40.0 25.8 %shard_map.138 = (bf16[32,32,256]{2,1,0:T(8,128)(2,1)}, bf16[1,256,256]{2,1,0:T(8,128)(2,1)}, f32[1,2,256]{2,1,0:T(2,128)}, bf16[1,256,256]{2,1,0:T(8,128)(2,1)}, f32[1,2,256]{2,1,0:T(2,128)}) custom-call(s32[32]{0:T(128)} %table.3, bf16[32,32,256]{2,1,0:T(8,128)(2,1)} %get-tuple-element.10.got, bf16[1,256,256]{2,1,0:T(8,128)(2,1)} %get-tuple-element.11.refs_0_, ...), custom_call_target="tpu_custom_call" | custom-call | tf_op jit(solution)/shard_map/pallas_call | solution.py:419

commit v3 on v2

v3 whole, which is shorter than its diff:
```python
import functools

import jax
import jax.numpy as jnp
from jax import lax
from jax.experimental import pallas as pl
from jax.experimental.pallas import tpu as pltpu
from jax.sharding import PartitionSpec as P

QG = 128
DECAY = 0.9
EPSILON = 1e-06
VMEM_BYTES = 64 * 1024 * 1024
MESH = pl.DeviceIdType.MESH
F32 = jnp.float32
BF16 = jnp.bfloat16


def kernel(
    shards,
    copies,
    cuts,
    table,
    grads_hbm,
    lc_hbm,
    ls_hbm,
    rc_hbm,
    rs_hbm,
    lrc_hbm,
    lrs_hbm,
    rrc_hbm,
    rrs_hbm,
    got,
    new_left,
    new_left_scale,
    new_right,
    new_right_scale,
    grads,
    lc,
    ls,
    rc,
    rs,
    lrc,
    lrs,
    rrc,
    rrs,
    packed,
    relayed,
    pieces,
    moved,
    in_sem,
    relay_send,
    relay_recv,
    a_send,
    a_recv,
    b_send,
    b_recv,
    f_send,
):
    me_s = lax.axis_index("shard")
    me_r = lax.axis_index("replica")
    rows = grads.shape[1]
    order = lc.shape[1]
    blocks = shards * copies
    size = shards // cuts
    in_line = copies == 4

    loads = []
    for k, (src, dst) in enumerate(
        [
            (grads_hbm.at[0], grads),
            (lrc_hbm, lrc),
            (lrs_hbm, lrs),
            (rrc_hbm, rrc),
            (rrs_hbm, rrs),
            (lc_hbm, lc),
            (ls_hbm, ls),
            (rc_hbm, rc),
            (rs_hbm, rs),
        ]
    ):
        copy = pltpu.make_async_copy(src, dst, in_sem.at[k])
        copy.start()
        loads.append(copy)

    def device(k):
        return (lax.rem(k, shards), k // shards)

    me = me_r * shards + me_s
    barrier = pltpu.get_barrier_semaphore()

    def greet(d, carry):
        pl.semaphore_signal(
            barrier, inc=1, device_id=device(lax.rem(me + d, blocks)), device_id_type=MESH
        )
        return carry

    lax.fori_loop(1, blocks, greet, 0, unroll=True if in_line else 1)

    loads[0].wait()

    def pack(k, carry):
        packed[k] = grads[table[lax.rem(k, shards) * copies + k // shards]]
        return carry

    lax.fori_loop(0, blocks, pack, 0, unroll=8)
    pl.semaphore_wait(barrier, blocks - 1)

    partner = me_r + 1 - 2 * lax.rem(me_r, 2)
    opposite = copies - 1 - me_r
    across = copies - 1 - partner
    is_end = jnp.logical_or(me_r == 0, me_r == copies - 1)
    is_mid = jnp.logical_not(is_end)
    kinds = pieces.shape[0]

    def group(r, c):
        return pl.ds(r * shards + c * size, size)

    def a_copy(src, kind, k, to_s, to_r):
        return pltpu.make_async_remote_copy(
            src_ref=src,
            dst_ref=pieces.at[kind, me_s],
            send_sem=a_send.at[k, to_s],
            recv_sem=a_recv.at[kind, me_s],
            device_id=(to_s, to_r),
            device_id_type=MESH,
        )

    def own_a(k, to_s, to_r, kind):
        return a_copy(packed.at[to_r * shards + to_s], kind, k, to_s, to_r)

    def a_arrival(kind, source):
        return pltpu.make_async_remote_copy(
            src_ref=packed.at[source],
            dst_ref=pieces.at[kind, source],
            send_sem=a_send.at[0, source],
            recv_sem=a_recv.at[kind, source],
            device_id=(source, partner if in_line else lax.rem(me_r + 1, copies)),
            device_id_type=MESH,
        )

    def relay_copy(k, c):
        return pltpu.make_async_remote_copy(
            src_ref=packed.at[group([across, opposite][k], c)],
            dst_ref=relayed.at[k, pl.ds(c * size, size)],
            send_sem=relay_send.at[k, c],
            recv_sem=relay_recv.at[k, c],
            device_id=(me_s, partner),
            device_id_type=MESH,
        )

    def pair_a(k, to_s):
        return a_copy(relayed.at[k, to_s], 2, 2 + k, to_s, [opposite, across][k])

    def relay(k):
        for c in range(cuts):
            relay_copy(k, c).wait_recv()
            at = pl.ds(c * size, size)
            own = packed[group([opposite, across][k], c)].astype(F32)
            relayed[k, at] = (relayed[k, at].astype(F32) + own).astype(BF16)
            for n in range(size):
                pair_a(k, c * size + lax.rem(me_s + n, size)).start()

    around = [lax.rem(me_s + d, shards) for d in range(shards)]
    OWN, DIRECT = 0, 1

    if in_line:

        @pl.when(is_end)
        def _():
            for c in range(cuts):
                relay_copy(0, c).start()
            for s in around:
                own_a(1, s, partner, DIRECT).start()
            for c in range(cuts):
                relay_copy(1, c).start()
            for s in around[1:]:
                own_a(0, s, me_r, OWN).start()

        @pl.when(is_mid)
        def _():
            for s in around[1:]:
                own_a(0, s, me_r, OWN).start()
            for s in around:
                own_a(1, s, partner, DIRECT).start()
            relay(0)

        pieces[OWN, me_s] = packed[me]
    else:

        def all_a(d, act):
            to_s, to_r = device(lax.rem(me + d, blocks))
            act(own_a(to_r, to_s, to_r, me_r))

        def start_a(d, carry):
            all_a(d, lambda copy: copy.start())
            return carry

        lax.fori_loop(1, blocks, start_a, 0)
        pieces[me_r, me_s] = packed[me]

    for copy in loads[1:]:
        copy.wait()
    zeros = jnp.zeros((2, order), F32)
    columns = jnp.concatenate([ls[0], rs[0], lrs[0], zeros], axis=0).T

    if in_line:
        for s in around[1:]:
            a_arrival(OWN, s).wait_recv()
        for kind in (1, 2):
            for s in around:
                a_arrival(kind, s).wait_recv()
    else:

        def await_a(d, carry):
            source, kind = device(lax.rem(me + d, blocks))
            a_arrival(kind, source).wait_recv()
            return carry

        lax.fori_loop(1, blocks, await_a, 0)

    summed32 = pieces[0].astype(F32)
    for kind in range(1, kinds):
        summed32 = summed32 + pieces[kind].astype(F32)
    summed32 = summed32.reshape(order, order)
    summed = summed32.astype(BF16)
    half = columns[:, 4:5] * jnp.dot(lrc[0, :, :QG], summed[:QG], preferred_element_type=F32)
    half = half + columns[:, 5:6] * jnp.dot(
        lrc[0, :, QG:], summed[QG:], preferred_element_type=F32
    )
    product = jnp.concatenate(
        [
            jnp.dot(
                (half * rrs[0, g : g + 1]).astype(BF16),
                rrc[0, :, g * QG : (g + 1) * QG],
                preferred_element_type=F32,
            )
            for g in range(order // QG)
        ],
        axis=1,
    )
    count = 1.0 / (order * order)
    grad_power = jnp.sum(jnp.sum(summed32 * summed32, axis=0, keepdims=True), axis=1, keepdims=True)
    prod_power = jnp.sum(jnp.sum(product * product, axis=0, keepdims=True), axis=1, keepdims=True)
    ratio = jnp.sqrt(grad_power * count + EPSILON) / jnp.sqrt(prod_power * count + EPSILON)
    moved[...] = (product * ratio).reshape(shards, rows, order).astype(BF16)

    def b_copy(k, to_s, to_r):
        return pltpu.make_async_remote_copy(
            src_ref=moved.at[to_s],
            dst_ref=got.at[me],
            send_sem=b_send.at[k, to_s],
            recv_sem=b_recv.at[me],
            device_id=(to_s, to_r),
            device_id_type=MESH,
        )

    def forward(k, s):
        at = [opposite, across][k] * shards + s
        return pltpu.make_async_remote_copy(
            src_ref=got.at[at],
            dst_ref=got.at[at],
            send_sem=f_send.at[k, s],
            recv_sem=b_recv.at[at],
            device_id=(me_s, partner),
            device_id_type=MESH,
        )

    def b_arrival(r, s):
        at = r * shards + s
        return pltpu.make_async_remote_copy(
            src_ref=got.at[at],
            dst_ref=got.at[at],
            send_sem=b_send.at[0, s],
            recv_sem=b_recv.at[at],
            device_id=(me_s, partner if in_line else lax.rem(me_r + 1, copies)),
            device_id_type=MESH,
        )

    if in_line:

        @pl.when(is_end)
        def _():
            for s in around:
                b_copy(2, s, across).start()
            for d, s in enumerate(around):
                b_copy(1, s, partner).start()
                if d:
                    b_copy(0, s, me_r).start()

        @pl.when(is_mid)
        def _():
            for s in around:
                b_copy(1, s, partner).start()
            relay(1)
            for d, s in enumerate(around):
                b_copy(2, s, opposite).start()
                if d:
                    b_copy(0, s, me_r).start()

    else:

        def start_b(d, carry):
            to_s, to_r = device(lax.rem(me + d, blocks))
            b_copy(to_r, to_s, to_r).start()
            return carry

        lax.fori_loop(1, blocks, start_b, 0)
    got[me] = moved[me_s]

    lane = lax.broadcasted_iota(jnp.int32, (order, QG), 1)

    def statistic(k, code, contracted, out, steps):
        gram = lax.dot_general(
            summed, summed, (((contracted,), (contracted,)), ((), ())), preferred_element_type=F32
        )
        for g in range(order // QG):
            at = 2 * k + g
            cols = slice(g * QG, (g + 1) * QG)
            old = code[0, :, cols].astype(F32) * columns[:, at : at + 1]
            new = DECAY * old + (1.0 - DECAY) * gram[:, cols]
            step = (jnp.max(jnp.abs(new), axis=1, keepdims=True) + EPSILON) / 7.0
            out[0, :, cols] = (new * (1.0 / step)).astype(BF16)
            steps = jnp.where(lane == at, step, steps)
        return steps

    steps = statistic(0, lc, 1, new_left, jnp.zeros((order, QG), F32))

    steps = statistic(1, rc, 0, new_right, steps)
    flipped = steps.T
    new_left_scale[0] = flipped[0:2]
    new_right_scale[0] = flipped[2:4]

    if in_line:

        @pl.when(is_mid)
        def _():
            for k, r in enumerate([opposite, across]):
                for s in around:
                    b_arrival(r, s).wait_recv()
                    forward(k, s).start()
            for s in around:
                own_a(1, s, partner, DIRECT).wait_send()
                b_copy(1, s, partner).wait_send()
                b_copy(2, s, opposite).wait_send()
                for k in range(2):
                    pair_a(k, s).wait_send()
                    forward(k, s).wait_send()

        @pl.when(is_end)
        def _():
            for r in (opposite, across):
                for s in around:
                    b_arrival(r, s).wait_recv()
            for s in around:
                own_a(1, s, partner, DIRECT).wait_send()
                b_copy(1, s, partner).wait_send()
                b_copy(2, s, across).wait_send()
            for k in range(2):
                for c in range(cuts):
                    relay_copy(k, c).wait_send()

        for s in around:
            b_arrival(partner, s).wait_recv()
        for s in around[1:]:
            b_arrival(me_r, s).wait_recv()
            own_a(0, s, me_r, OWN).wait_send()
            b_copy(0, s, me_r).wait_send()
    else:

        def finish(d, carry):
            to_s, to_r = device(lax.rem(me + d, blocks))
            b_arrival(to_r, to_s).wait_recv()
            all_a(d, lambda copy: copy.wait_send())
            b_copy(to_r, to_s, to_r).wait_send()
            return carry

        lax.fori_loop(1, blocks, finish, 0)


def place(shards, copies, table, got, *refs):
    stats, direction, outs, sem = refs[:4], refs[4], refs[5:9], refs[9]
    others = [
        pltpu.make_async_copy(src, dst, sem.at[1 + k])
        for k, (src, dst) in enumerate(zip(stats, outs))
    ]
    for copy in others:
        copy.start()

    def put(k, carry):
        block = table[lax.rem(k, shards) * copies + k // shards]
        pltpu.make_async_copy(got.at[k], direction.at[block], sem.at[0]).start()
        return carry

    lax.fori_loop(0, shards * copies, put, 0, unroll=8)
    pltpu.make_async_copy(got, direction, sem.at[0]).wait()
    for copy in others:
        copy.wait()


def local(shards, copies, grads, table, *factors):
    blocks, rows, order = grads.shape[1:]
    cuts = 4
    vmem = pl.BlockSpec(memory_space=pltpu.VMEM)
    smem = pl.BlockSpec(memory_space=pltpu.SMEM)
    hbm = pl.BlockSpec(memory_space=pltpu.HBM)
    code = jax.ShapeDtypeStruct((1, order, order), BF16)
    scale = jax.ShapeDtypeStruct((1, order // QG, order), F32)
    outs = [jax.ShapeDtypeStruct((blocks, rows, order), BF16), code, scale, code, scale]
    dma = pltpu.SemaphoreType.DMA
    results = pl.pallas_call(
        functools.partial(kernel, shards, copies, cuts),
        out_shape=outs,
        in_specs=[smem] + [hbm] * 9,
        out_specs=[vmem] * 5,
        scratch_shapes=[pltpu.VMEM((blocks, rows, order), BF16)]
        + [pltpu.VMEM(f.shape, f.dtype) for f in factors]
        + [
            pltpu.VMEM((blocks, rows, order), BF16),
            pltpu.VMEM((2, shards, rows, order), BF16),
            pltpu.VMEM((3 if copies == 4 else copies, shards, rows, order), BF16),
            pltpu.VMEM((shards, rows, order), BF16),
            dma((9,)),
            dma((2, cuts)),
            dma((2, cuts)),
            dma((copies, shards)),
            dma((copies, shards)),
            dma((copies, shards)),
            dma((blocks,)),
            dma((2, shards)),
        ],
        compiler_params=pltpu.CompilerParams(
            collective_id=0, has_side_effects=True, vmem_limit_bytes=VMEM_BYTES
        ),
    )(table, grads, *factors)
    return pl.pallas_call(
        functools.partial(place, shards, copies),
        out_shape=outs,
        in_specs=[smem] + [vmem] * 5,
        out_specs=[hbm] * 5,
        scratch_shapes=[dma((5,))],
        compiler_params=pltpu.CompilerParams(vmem_limit_bytes=VMEM_BYTES),
    )(table, *results)


def solution(mesh):
    slots = P(("shard", "replica"), None, None)
    return jax.shard_map(
        functools.partial(local, mesh.shape["shard"], mesh.shape["replica"]),
        mesh=mesh,
        in_specs=(P("replica", None, "shard", None), P()) + (slots,) * 8,
        out_specs=(P(None, "shard", None), slots, slots, slots, slots),
        check_vma=False,
    )
```

time: 66 us -> 37.9 us (0.57)
  Pallas kernels: 65.2 us -> 37.1 us
    pallas_call x1, Pallas kernels: 25.8 us -> 2.11 us  [local(): pl.pallas_call(functools.partial(place, shards, copies), out_shape=outs,...]
    pallas_call x1, Pallas kernels: 39.4 us -> 34.9 us  [local(): pl.pallas_call(functools.partial(kernel, shards, copies, cuts), out_shape...]
where the time goes in v3:
time: 37.9 us; the launch traced here: 37.7 us
  Pallas kernels  37.1 us (98%)
  between operations  0.64 us (2%)
    pallas_call x1, Pallas kernels, local(): pl.pallas_call(functools.partial(kernel, shards, copies, cuts), out_shape...  34.9 us
    pallas_call x1, Pallas kernels, local(): pl.pallas_call(functools.partial(place, shards, copies), out_shape=outs,...  2.11 us

profile of v3, /device:TPU:0, one launch (start us, length us, event | category | flops | bytes accessed | tf_op | source)
XLA Modules:
  0.0 37.7 jit_solution(4741031854126136584)
XLA Ops:
  0.6 34.9 %shard_map.137 = (bf16[32,32,256]{2,1,0:T(8,128)(2,1)}, bf16[1,256,256]{2,1,0:T(8,128)(2,1)}, f32[1,2,256]{2,1,0:T(2,128)}, bf16[1,256,256]{2,1,0:T(8,128)(2,1)}, f32[1,2,256]{2,1,0:T(2,128)}) custom-call(s32[32]{0:T(128)} %table.3, bf16[1,32,32,256]{3,2,1,0:T(8,128)(2,1)} %grads_hbm.1, bf16[1,256,256]{2,1,0:T(8,128)(2,1)} %lc_hbm.1, f32[1,2,256]{2,1,0:T(2,128)} %ls_hbm.1, ...), custom_call_target="tpu_custom_call" | custom-call | tf_op jit(solution)/shard_map/pallas_call | solution.py:411
  35.6 2.1 %shard_map.138 = (bf16[32,32,256]{2,1,0:T(8,128)(2,1)}, bf16[1,256,256]{2,1,0:T(8,128)(2,1)}, f32[1,2,256]{2,1,0:T(2,128)}, bf16[1,256,256]{2,1,0:T(8,128)(2,1)}, f32[1,2,256]{2,1,0:T(2,128)}) custom-call(s32[32]{0:T(128)} %table.3, bf16[32,32,256]{2,1,0:T(8,128)(2,1)} %get-tuple-element.10.got, bf16[1,256,256]{2,1,0:T(8,128)(2,1)} %get-tuple-element.11.refs_0_, ...), custom_call_target="tpu_custom_call" | custom-call | tf_op jit(solution)/shard_map/pallas_call | solution.py:436

commit v4 on v3

--- a/solution.py
+++ b/solution.py
@@ -30,11 +30,11 @@
     lrs_hbm,
     rrc_hbm,
     rrs_hbm,
-    got,
-    new_left,
-    new_left_scale,
-    new_right,
-    new_right_scale,
+    got_hbm,
+    new_left_hbm,
+    new_left_scale_hbm,
+    new_right_hbm,
+    new_right_scale_hbm,
     grads,
     lc,
     ls,
@@ -48,7 +48,13 @@
     relayed,
     pieces,
     moved,
+    got,
+    new_left,
+    new_left_scale,
+    new_right,
+    new_right_scale,
     in_sem,
+    out_sem,
     relay_send,
     relay_recv,
     a_send,
@@ -181,9 +187,9 @@
         def _():
             for s in around[1:]:
                 own_a(0, s, me_r, OWN).start()
+            relay(0)
             for s in around:
                 own_a(1, s, partner, DIRECT).start()
-            relay(0)
 
         pieces[OWN, me_s] = packed[me]
     else:
@@ -283,18 +289,18 @@
         def _():
             for s in around:
                 b_copy(2, s, across).start()
+            for s in around:
+                b_copy(1, s, partner).start()
+            for s in around[1:]:
+                b_copy(0, s, me_r).start()
+
+        @pl.when(is_mid)
+        def _():
+            relay(1)
+            for s in around:
+                b_copy(2, s, opposite).start()
             for d, s in enumerate(around):
                 b_copy(1, s, partner).start()
-                if d:
-                    b_copy(0, s, me_r).start()
-
-        @pl.when(is_mid)
-        def _():
-            for s in around:
-                b_copy(1, s, partner).start()
-            relay(1)
-            for d, s in enumerate(around):
-                b_copy(2, s, opposite).start()
                 if d:
                     b_copy(0, s, me_r).start()
 
@@ -330,8 +336,28 @@
     flipped = steps.T
     new_left_scale[0] = flipped[0:2]
     new_right_scale[0] = flipped[2:4]
+    stores = []
+    for k, (src, dst) in enumerate(
+        [
+            (new_left, new_left_hbm),
+            (new_left_scale, new_left_scale_hbm),
+            (new_right, new_right_hbm),
+            (new_right_scale, new_right_scale_hbm),
+        ]
+    ):
+        copy = pltpu.make_async_copy(src, dst, out_sem.at[copies + k])
+        copy.start()
+        stores.append(copy)
+
+    def store(r):
+        at = pl.ds(r * shards, shards)
+        return pltpu.make_async_copy(got.at[at], got_hbm.at[at], out_sem.at[r])
+
 
     if in_line:
+        for s in around[1:]:
+            b_arrival(me_r, s).wait_recv()
+        store(me_r).start()
 
         @pl.when(is_mid)
         def _():
@@ -339,6 +365,21 @@
                 for s in around:
                     b_arrival(r, s).wait_recv()
                     forward(k, s).start()
+                store(r).start()
+
+        for s in around:
+            b_arrival(partner, s).wait_recv()
+        store(partner).start()
+
+        @pl.when(is_end)
+        def _():
+            for r in (across, opposite):
+                for s in around:
+                    b_arrival(r, s).wait_recv()
+                store(r).start()
+
+        @pl.when(is_mid)
+        def _():
             for s in around:
                 own_a(1, s, partner, DIRECT).wait_send()
                 b_copy(1, s, partner).wait_send()
@@ -349,9 +390,6 @@
 
         @pl.when(is_end)
         def _():
-            for r in (opposite, across):
-                for s in around:
-                    b_arrival(r, s).wait_recv()
             for s in around:
                 own_a(1, s, partner, DIRECT).wait_send()
                 b_copy(1, s, partner).wait_send()
@@ -360,10 +398,7 @@
                 for c in range(cuts):
                     relay_copy(k, c).wait_send()
 
-        for s in around:
-            b_arrival(partner, s).wait_recv()
         for s in around[1:]:
-            b_arrival(me_r, s).wait_recv()
             own_a(0, s, me_r, OWN).wait_send()
             b_copy(0, s, me_r).wait_send()
     else:
@@ -376,6 +411,12 @@
             return carry
 
         lax.fori_loop(1, blocks, finish, 0)
+        for r in range(copies):
+            store(r).start()
+    for r in range(copies):
+        store(r).wait()
+    for copy in stores:
+        copy.wait()
 
 
 def place(shards, copies, table, got, *refs):
@@ -401,18 +442,18 @@
 def local(shards, copies, grads, table, *factors):
     blocks, rows, order = grads.shape[1:]
     cuts = 4
-    vmem = pl.BlockSpec(memory_space=pltpu.VMEM)
     smem = pl.BlockSpec(memory_space=pltpu.SMEM)
     hbm = pl.BlockSpec(memory_space=pltpu.HBM)
     code = jax.ShapeDtypeStruct((1, order, order), BF16)
     scale = jax.ShapeDtypeStruct((1, order // QG, order), F32)
     outs = [jax.ShapeDtypeStruct((blocks, rows, order), BF16), code, scale, code, scale]
     dma = pltpu.SemaphoreType.DMA
+    held = [pltpu.VMEM(o.shape, o.dtype) for o in outs]
     results = pl.pallas_call(
         functools.partial(kernel, shards, copies, cuts),
         out_shape=outs,
         in_specs=[smem] + [hbm] * 9,
-        out_specs=[vmem] * 5,
+        out_specs=[hbm] * 5,
         scratch_shapes=[pltpu.VMEM((blocks, rows, order), BF16)]
         + [pltpu.VMEM(f.shape, f.dtype) for f in factors]
         + [
@@ -420,7 +461,11 @@
             pltpu.VMEM((2, shards, rows, order), BF16),
             pltpu.VMEM((3 if copies == 4 else copies, shards, rows, order), BF16),
             pltpu.VMEM((shards, rows, order), BF16),
+        ]
+        + held
+        + [
             dma((9,)),
+            dma((copies + 4,)),
             dma((2, cuts)),
             dma((2, cuts)),
             dma((copies, shards)),
@@ -436,7 +481,7 @@
     return pl.pallas_call(
         functools.partial(place, shards, copies),
         out_shape=outs,
-        in_specs=[smem] + [vmem] * 5,
+        in_specs=[smem] + [pl.BlockSpec(memory_space=pltpu.VMEM)] * 5,
         out_specs=[hbm] * 5,
         scratch_shapes=[dma((5,))],
         compiler_params=pltpu.CompilerParams(vmem_limit_bytes=VMEM_BYTES),

time: 37.9 us -> 37.5 us (0.989)
  Pallas kernels: 37.1 us -> 36.7 us
where the time goes in v4:
time: 37.5 us; the launch traced here: 37.4 us
  Pallas kernels  36.7 us (98%)
  between operations  0.64 us (2%)
    pallas_call x1, Pallas kernels, local(): pl.pallas_call(functools.partial(kernel, shards, copies, cuts), out_shape...  34.6 us
    pallas_call x1, Pallas kernels, local(): pl.pallas_call(functools.partial(place, shards, copies), out_shape=outs,...  2.11 us

profile of v4, /device:TPU:0, one launch (start us, length us, event | category | flops | bytes accessed | tf_op | source)
XLA Modules:
  0.0 37.4 jit_solution(2170322608886955028)
XLA Ops:
  0.6 34.6 %shard_map.137 = (bf16[32,32,256]{2,1,0:T(8,128)(2,1)}, bf16[1,256,256]{2,1,0:T(8,128)(2,1)}, f32[1,2,256]{2,1,0:T(2,128)}, bf16[1,256,256]{2,1,0:T(8,128)(2,1)}, f32[1,2,256]{2,1,0:T(2,128)}) custom-call(s32[32]{0:T(128)} %table.3, bf16[1,32,32,256]{3,2,1,0:T(8,128)(2,1)} %grads_hbm.1, bf16[1,256,256]{2,1,0:T(8,128)(2,1)} %lc_hbm.1, f32[1,2,256]{2,1,0:T(2,128)} %ls_hbm.1, ...), custom_call_target="tpu_custom_call" | custom-call | tf_op jit(solution)/shard_map/pallas_call | solution.py:452
  35.3 2.1 %shard_map.138 = (bf16[32,32,256]{2,1,0:T(8,128)(2,1)}, bf16[1,256,256]{2,1,0:T(8,128)(2,1)}, f32[1,2,256]{2,1,0:T(2,128)}, bf16[1,256,256]{2,1,0:T(8,128)(2,1)}, f32[1,2,256]{2,1,0:T(2,128)}) custom-call(s32[32]{0:T(128)} %table.3, bf16[32,32,256]{2,1,0:T(8,128)(2,1)} %get-tuple-element.10.got, bf16[1,256,256]{2,1,0:T(8,128)(2,1)} %get-tuple-element.11.refs_0_, ...), custom_call_target="tpu_custom_call" | custom-call | tf_op jit(solution)/shard_map/pallas_call | solution.py:481
